TPU v7x, 128 devices: a whole 4x4x4 slice. The times are simulated.
128 devices in a mesh: face: 8 (over z_lo, x), tile: 16 (over z_hi, y, core).
Axes of the slice: x: 4, y: 4, z: 4 (z_hi: 2, z_lo: 2; z = z_hi * 2 + z_lo), core: 2. Of those that a mesh axis runs over, the one named last changes fastest.
Arguments:
- source: bfloat16 [8192, 16, 128], P(('face', 'tile')), may hold values from -6 to 6
- entry_block: int32 [16384], P(('face', 'tile')), may hold values from 0 to 16383, as said below
- entry_source: int32 [16384], P(('face', 'tile')), may hold values from 0 to 63
- entry_weight: bfloat16 [16384, 128, 128], P(('face', 'tile')), may hold values from -0.5 to 0.5
- lat_to_nested: int32 [16384], P(('face', 'tile')), may hold values from 0 to 16383, as said below
- face_links: int32 [8, 4, 3], replicated, may hold values from 0 to 7, as said below
- w_in: bfloat16 [16, 90], replicated, may hold values from -1.5 to 1.5
- b_in: float32 [90], replicated, may hold values from -3 to 3
- kernel: float32 [9, 90], replicated, may hold values from -2 to 2
- ln_gain: float32 [90], replicated, may hold values from 0.1 to 1.9
- ln_bias: float32 [90], replicated, may hold values from -3 to 3
- w_one: bfloat16 [90, 360], replicated, may hold values from -0.625 to 0.625
- b_one: float32 [360], replicated, may hold values from -3 to 3
- w_two: bfloat16 [360, 90], replicated, may hold values from -0.3125 to 0.3125
- b_two: float32 [90], replicated, may hold values from -3 to 3
- cotangent: bfloat16 [8, 90, 512, 512], P('face', None, 'tile'), may hold values from -6 to 6
Outputs:
- output: bfloat16 [8, 90, 512, 512], P('face', None, 'tile')
- grad_one: float32 [90, 360], replicated
- grad_two: float32 [360, 90], replicated
- grad_kernel: float32 [9, 90], replicated
Inputs may be any that keep to these rules, and one draw needn't show every extreme that they name: `entry_block`: blocks k * 128 to (k + 1) * 128 - 1 belong to device k. At most 2 entries of one device name blocks of one device; in every draw one device gets exactly 2 from every device. `lat_to_nested`: A permutation of all blocks; the 128 blocks of each device go one to each device. `face_links`: entry [f, s, 0] names a face other than f; [f, s, 1] a side 0 to 3; [f, s, 2] is 0 or 1.
All inputs are finite; a program needn't handle non-finite values.
Results may differ from a plain program's by a relative error of at most 0.0081.
Values may be sent and summed in bfloat16 or wider, within the bound.
A program may use at most 192 MiB of HBM per device.

v0:
```python
import math
import jax
import jax.numpy as jnp
from jax import lax
from jax.sharding import PartitionSpec as P

CAP = 2
GELU_K = 0.7978845608028654
GELU_C = 0.044715
NORM_EPS = 1e-06


def with_halo(cells, sides, width):
    for axis, dim in sides:
        count = lax.axis_size(axis)
        ends = count - 1
        head = lax.slice_in_dim(cells, 0, width, axis=dim)
        tail = lax.slice_in_dim(cells, cells.shape[dim] - width, cells.shape[dim], axis=dim)
        cells = jnp.concatenate(
            [
                lax.ppermute(tail, axis, [(i, (i + 1) % count) for i in range(ends)]),
                cells,
                lax.ppermute(head, axis, [((i + 1) % count, i) for i in range(ends)]),
            ],
            axis=dim,
        )
    return cells


def gelu_pair(pre_act):
    inner = GELU_K * (pre_act + GELU_C * pre_act * pre_act * pre_act)
    tanh_val = jnp.tanh(inner)
    gelu_val = 0.5 * pre_act * (1.0 + tanh_val)
    gelu_slope = 0.5 * (1.0 + tanh_val) + 0.5 * pre_act * (1.0 - tanh_val * tanh_val) * GELU_K * (
        1.0 + 3.0 * GELU_C * pre_act * pre_act
    )
    return (gelu_val, gelu_slope)


def contract_rows(left_mat, right_mat):
    return lax.dot_general(
        left_mat, right_mat, (((1,), (1,)), ((), ())), preferred_element_type=jnp.float32
    )


def strip_work(padded, middle, cotan, kernel, ln_gain, ln_bias, w_one, b_one, w_two, b_two, scale):
    lat_count = padded.shape[0]
    row_count = padded.shape[1] - 2
    col_count = padded.shape[2] - 2
    wide = padded.astype(jnp.float32)
    depth_sum = jnp.zeros((lat_count, row_count, col_count), jnp.float32)
    for tap_index in range(9):
        row_off = tap_index // 3
        col_off = tap_index % 3
        window = wide[:, row_off : row_off + row_count, col_off : col_off + col_count]
        depth_sum = depth_sum + kernel[tap_index][:, None, None] * window
    flat = depth_sum.reshape(lat_count, row_count * col_count)
    mean_val = jnp.mean(flat, axis=0, keepdims=True)
    centered = flat - mean_val
    variance = jnp.mean(centered * centered, axis=0, keepdims=True)
    inv_std = lax.rsqrt(variance + NORM_EPS)
    scaled = centered * inv_std
    normed = (scaled * ln_gain[:, None] + ln_bias[:, None]).astype(jnp.bfloat16)
    pre_act = jnp.dot(w_one.T, normed, preferred_element_type=jnp.float32) + b_one[:, None]
    gelu_val, gelu_slope = gelu_pair(pre_act)
    hidden = gelu_val.astype(jnp.bfloat16)
    summed = (
        jnp.dot(w_two.T, hidden, preferred_element_type=jnp.float32)
        + b_two[:, None]
        + middle.reshape(lat_count, -1).astype(jnp.float32)
    )
    output = summed.astype(jnp.bfloat16).reshape(lat_count, row_count, col_count)
    cot_flat = cotan.reshape(lat_count, -1)
    grad_two = contract_rows(hidden, cot_flat) * scale
    back_hidden = jnp.dot(w_two, cot_flat, preferred_element_type=jnp.float32)
    back_pre = (back_hidden * gelu_slope).astype(jnp.bfloat16)
    grad_one = contract_rows(normed, back_pre) * scale
    back_hat = jnp.dot(w_one, back_pre, preferred_element_type=jnp.float32) * ln_gain[:, None]
    back_depth = inv_std * (
        back_hat
        - jnp.mean(back_hat, axis=0, keepdims=True)
        - scaled * jnp.mean(back_hat * scaled, axis=0, keepdims=True)
    )
    back_grid = back_depth.reshape(lat_count, row_count, col_count)
    kernel_rows = []
    for tap_index in range(9):
        row_off = tap_index // 3
        col_off = tap_index % 3
        window = wide[:, row_off : row_off + row_count, col_off : col_off + col_count]
        kernel_rows.append(jnp.sum(back_grid * window, axis=(1, 2)))
    grad_kernel = jnp.stack(kernel_rows, axis=0) * scale
    return (output, grad_one, grad_two, grad_kernel)


def lift(w_in, b_in, values):
    flat = values.reshape(values.shape[0], -1)
    mixed = jnp.dot(w_in.T, flat, preferred_element_type=jnp.float32) + b_in[:, None]
    return mixed.astype(jnp.bfloat16).reshape((w_in.shape[1],) + values.shape[1:])


def assemble(rows_part, cols_part):
    tile_count = rows_part.shape[0]
    chan_count = rows_part.shape[1]
    left_line = cols_part[:, 0].transpose(1, 0, 2).reshape(chan_count, -1)
    right_line = cols_part[:, 1].transpose(1, 0, 2).reshape(chan_count, -1)
    return jnp.stack([rows_part[0], rows_part[tile_count - 1], left_line, right_line], axis=0)


def per_device(
    source,
    entry_block,
    entry_source,
    entry_weight,
    lat_to_nested,
    face_links,
    w_in,
    b_in,
    kernel,
    ln_gain,
    ln_bias,
    w_one,
    b_one,
    w_two,
    b_two,
    cotangent,
):
    tile_count = lax.axis_size("tile")
    tile_at = lax.axis_index("tile")
    face_at = lax.axis_index("face")
    face_count = lax.axis_size("face")
    dev_count = lax.axis_size(("face", "tile"))
    in_count = source.shape[1]
    block_len = entry_weight.shape[2]
    row_count = cotangent.shape[2]
    line_len = cotangent.shape[3]
    chosen = jnp.take(source, entry_source, axis=0)
    partials = jnp.einsum(
        "eis,esp->eip", chosen, entry_weight, preferred_element_type=jnp.float32
    ).astype(jnp.bfloat16)
    owner_dev = entry_block // dev_count
    local_block = entry_block % dev_count
    hit_table = (owner_dev[:, None] == jnp.arange(dev_count, dtype=jnp.int32)[None, :]).astype(
        jnp.int32
    )
    slot_rank = jnp.sum((jnp.cumsum(hit_table, axis=0) - 1) * hit_table, axis=1)
    outbox = (
        jnp.zeros((dev_count, CAP, in_count, block_len), jnp.bfloat16)
        .at[owner_dev, slot_rank]
        .set(partials)
    )
    labels = (
        jnp.full((dev_count, CAP), dev_count, jnp.int32).at[owner_dev, slot_rank].set(local_block)
    )
    received, got_labels = (
        lax.all_to_all(outbox, ("face", "tile"), split_axis=0, concat_axis=0, tiled=True),
        lax.all_to_all(labels, ("face", "tile"), split_axis=0, concat_axis=0, tiled=True),
    )
    lat_sum = jnp.zeros((dev_count, in_count, block_len), jnp.float32)
    lat_sum = lat_sum.at[got_labels.reshape(-1)].add(
        received.reshape(-1, in_count, block_len).astype(jnp.float32), mode="drop"
    )
    lat_field = lat_sum.astype(jnp.bfloat16)
    target_dev = lat_to_nested // dev_count
    target_spot = lat_to_nested % dev_count
    outgoing = jnp.zeros_like(lat_field).at[target_dev].set(lat_field)
    out_spots = jnp.zeros((dev_count,), jnp.int32).at[target_dev].set(target_spot)
    incoming, in_spots = (
        lax.all_to_all(outgoing, ("face", "tile"), split_axis=0, concat_axis=0, tiled=True),
        lax.all_to_all(out_spots, ("face", "tile"), split_axis=0, concat_axis=0, tiled=True),
    )
    placed = jnp.zeros_like(incoming).at[in_spots].set(incoming)
    inputs_tile = placed.transpose(1, 0, 2).reshape(in_count, row_count, line_len)
    latent = lift(w_in, b_in, inputs_tile)
    chan_count = latent.shape[0]
    row_start = tile_at * row_count
    edge_cols = jnp.stack([latent[:, :, 0], latent[:, :, line_len - 1]], axis=0)
    edge_row = jnp.where(tile_at == 0, latent[:, 0, :], latent[:, row_count - 1, :])
    rows_face, cols_face = (
        lax.all_gather(edge_row.reshape(-1), "tile", axis=0, tiled=True),
        lax.all_gather(edge_cols.reshape(-1), "tile", axis=0, tiled=True),
    )
    own_lines = assemble(
        rows_face.reshape(tile_count, chan_count, line_len),
        cols_face.reshape(tile_count, 2, chan_count, row_count),
    )
    all_lines = lax.all_gather(own_lines.reshape(-1), "face", axis=0, tiled=True).reshape(
        face_count, 4, chan_count, line_len
    )
    face_link = face_links[face_at]
    picked = all_lines[face_link[:, 0], face_link[:, 1]]
    picked = jnp.where(face_link[:, 2][:, None, None] == 1, picked[:, :, ::-1], picked)
    row_lines = picked[0:2]
    full_cols = jnp.pad(picked[2:4], ((0, 0), (0, 0), (1, 1)))
    side_cols = lax.dynamic_slice_in_dim(full_cols, row_start, row_count + 2, 2)
    rim = jnp.stack([latent[:, 0, :], latent[:, row_count - 1, :]], axis=1)
    extended = with_halo(rim, (("tile", 1),), 1)
    upper_row = extended[:, 0, :]
    lower_row = extended[:, 3, :]
    spot_ids = jnp.arange(row_count + 2, dtype=jnp.int32) + row_start - 1
    inside = (spot_ids >= 0) & (spot_ids < line_len)
    side_cols = jnp.where(inside[None, None, :], side_cols, jnp.zeros_like(side_cols))
    top_row = jnp.where(tile_at == 0, row_lines[0], upper_row)
    bottom_row = jnp.where(tile_at == tile_count - 1, row_lines[1], lower_row)
    middle = jnp.concatenate([top_row[:, None, :], latent, bottom_row[:, None, :]], axis=1)
    padded = jnp.concatenate([side_cols[0][:, :, None], middle, side_cols[1][:, :, None]], axis=2)
    scale = 1.0 / math.sqrt(face_count * line_len * line_len)
    output, grad_one, grad_two, grad_kernel = strip_work(
        padded, latent, cotangent[0], kernel, ln_gain, ln_bias, w_one, b_one, w_two, b_two, scale
    )
    grad_one, grad_two, grad_kernel = lax.psum((grad_one, grad_two, grad_kernel), ("face", "tile"))
    return (output[None], grad_one, grad_two, grad_kernel)


def solution(mesh):
    placed = (
        P(("face", "tile"), None, None),
        P(("face", "tile")),
        P(("face", "tile")),
        P(("face", "tile"), None, None),
        P(("face", "tile")),
        P(),
        P(),
        P(),
        P(),
        P(),
        P(),
        P(),
        P(),
        P(),
        P(),
        P("face", None, "tile", None),
    )
    return jax.shard_map(
        per_device,
        mesh=mesh,
        in_specs=placed,
        out_specs=(P("face", None, "tile", None), P(), P(), P()),
        check_vma=False,
    )
```

profile of v0, /device:TPU:1, one launch (start us, length us, event | category | flops | bytes accessed | tf_op | source)
XLA Modules:
  0.0 591.9 jit_solution(9418654939937501962)
XLA Ops:
  8.4 6.4 %scatter_fusion = s32[128,2]{0,1:T(2,128)S(1)} fusion(s32[128,2]{0,1:T(2,128)S(1)} %broadcast_in_dim.44, s32[128]{0:T(128)S(1)} %fusion.33, s32[128]{0:T(128)S(1)} %get-tuple-element.43), kind=kCustom, calls=%fused_computation.3 | custom fusion | bytes 2560 | tf_op jit(solution)/shard_map/scatter | solution.py:152
  15.5 11.5 %all-to-all-start.1 = ((s32[128,1,2]{2,1,0:T(1,128)}), s32[128,1,2]{2,1,0:T(1,128)S(1)}, u32[]{:S(2)}, u32[]{:S(2)}) async-start(s32[128,1,2]{2,1,0:T(1,128)} %copy.79), calls=%async_computation.1 | async-start | bytes 131072 | tf_op jit(solution)/shard_map/all_to_all | solution.py:156
  33.0 13.3 %scatter_fusion.1 = bf16[128,2,16,128]{3,2,1,0:T(8,128)(2,1)} fusion(bf16[128,2,16,128]{3,2,1,0:T(8,128)(2,1)} %broadcast_in_dim.46, s32[128]{0:T(128)S(1)} %fusion.33, bf16[128,16,128]{2,1,0:T(8,128)(2,1)S(1)} %convolution_convert_fusion), kind=kCustom, calls=%fused_computation.4 | custom fusion | bytes 1573888 | tf_op jit(solution)/shard_map/scatter | solution.py:149
  46.2 9.8 %all-to-all-start.2 = ((bf16[128,2,16,128]{3,2,1,0:T(8,128)(2,1)}), bf16[128,2,16,128]{3,2,1,0:T(8,128)(2,1)S(1)}, u32[]{:S(2)}, u32[]{:S(2)}) async-start(bf16[128,2,16,128]{3,2,1,0:T(8,128)(2,1)} %scatter_fusion.1), calls=%async_computation.2 | async-start | bytes 2097152 | tf_op jit(solution)/shard_map/all_to_all | solution.py:155
  59.2 15.7 %all-to-all-done.2 = bf16[128,2,16,128]{3,2,1,0:T(8,128)(2,1)S(1)} async-done(((bf16[128,2,16,128]{3,2,1,0:T(8,128)(2,1)}), bf16[128,2,16,128]{3,2,1,0:T(8,128)(2,1)S(1)}, u32[]{:S(2)}, u32[]{:S(2)}) %all-to-all-start.2) | async-done | bytes 1048608 | tf_op jit(solution)/shard_map/all_to_all | solution.py:155
  74.9 4.5 all-to-all-start
  79.8 9.2 %scatter_fusion.2 = f32[128,16,128]{2,1,0:T(8,128)S(1)} fusion(f32[128,16,128]{2,1,0:T(8,128)S(1)} %broadcast_in_dim.43, s32[256]{0:T(256)S(1)} %bitcast.183, f32[256,16,128]{2,1,0:T(8,128)S(1)} %bitcast_convert_fusion), kind=kCustom, calls=%fused_computation.5 | custom fusion | flops 524288 | bytes 6292480 | tf_op jit(solution)/shard_map/scatter-add | solution.py:159
  90.0 13.2 %scatter_fusion.3 = bf16[128,16,128]{2,1,0:T(8,128)(2,1)} fusion(bf16[128,16,128]{2,1,0:T(8,128)(2,1)} %broadcast.194.clone, s32[128]{0:T(128)S(1)} %get-tuple-element.46, bf16[128,16,128]{2,1,0:T(8,128)(2,1)S(1)} %convert_element_type.45), kind=kCustom, calls=%fused_computation.6 | custom fusion | bytes 1573376 | tf_op jit(solution)/shard_map/scatter | solution.py:165
  103.1 9.8 %all-to-all-start.3 = ((bf16[128,16,128]{2,1,0:T(8,128)(2,1)}), bf16[128,16,128]{2,1,0:T(8,128)(2,1)S(1)}, u32[]{:S(2)}, u32[]{:S(2)}) async-start(bf16[128,16,128]{2,1,0:T(8,128)(2,1)} %scatter_fusion.3), calls=%async_computation.3 | async-start | bytes 1048576 | tf_op jit(solution)/shard_map/all_to_all | solution.py:168
  115.8 10.7 %all-to-all-done.3 = bf16[128,16,128]{2,1,0:T(8,128)(2,1)S(1)} async-done(((bf16[128,16,128]{2,1,0:T(8,128)(2,1)}), bf16[128,16,128]{2,1,0:T(8,128)(2,1)S(1)}, u32[]{:S(2)}, u32[]{:S(2)}) %all-to-all-start.3) | async-done | bytes 524320 | tf_op jit(solution)/shard_map/all_to_all | solution.py:168
  127.4 13.2 %scatter_fusion.4 = bf16[128,16,128]{2,1,0:T(8,128)(2,1)} fusion(bf16[128,16,128]{2,1,0:T(8,128)(2,1)} %broadcast.194, s32[128]{0:T(128)S(1)} %fusion.31, bf16[128,16,128]{2,1,0:T(8,128)(2,1)S(1)} %all-to-all-done.3), kind=kCustom, calls=%fused_computation.7 | custom fusion | bytes 1573376 | tf_op jit(solution)/shard_map/scatter | solution.py:171
  154.1 23.3 %all-gather = bf16[16,1,5760]{2,1,0:T(2,128)(2,1)} all-gather(bf16[1,1,5760]{2,1,0:T(2,128)(2,1)S(1)} %reshape.282), channel_id=1, replica_groups=mesh['face'=8,'tile'=16] {'tile'}, dimensions={0}, use_global_device_ids=true | all-gather | bytes 195840 | tf_op jit(solution)/shard_map/all_gather | solution.py:180
  185.9 4.6 all-gather.4.cloned.1.call-done
  201.0 3.7 copy.107
  205.1 3.8 slice.204
  214.0 24.0 %all-gather.6.cloned.1.call-done = bf16[1474560]{0:T(1024)(128)(2,1)} async-done(((bf16[184320]{0:T(1024)(128)(2,1)}), bf16[1474560]{0:T(1024)(128)(2,1)}) %all-gather.6.cloned.1.call-update) | async-done | bytes 2949136 | tf_op jit(solution)/shard_map/all_gather | solution.py:186
  238.0 5.6 reshape.217
  246.8 8.5 %rev.3 = bf16[4,90,512]{2,1,0:T(8,128)(2,1)} reverse(bf16[4,90,512]{2,1,0:T(8,128)(2,1)} %gather_fusion.1), dimensions={2} | reverse | bytes 737280 | tf_op jit(solution)/shard_map/rev | solution.py:191
  262.7 8.9 %maximum_convert_fusion = f32[90,34,514]{2,1,0:T(8,128)} fusion(bf16[90,34,1]{2,1,0:T(8,128)(2,1)} %copy.94, bf16[90,1,512]{2,1,0:T(2,128)(2,1)S(1)} %copy.91, bf16[90,32,512]{2,1,0:T(8,128)(2,1)} %slice.204, bf16[90,1,512]{2,1,0:T(2,128)(2,1)} %copy.90, bf16[90,34,1]{2,1,0:T(8,128)(2,1)} %copy.93), kind=kLoop, calls=%fused_computation.45 | loop fusion | flops 15728400 | bytes 9437040 | tf_op jit(solution)/shard_map/convert_element_type | solution.py:50
  271.6 34.9 %fusion.38 = (f32[32,512]{1,0:T(8,128)S(1)}, f32[90,32,512]{2,1,0:T(8,128)}) fusion(f32[90,34,514]{2,1,0:T(8,128)} %maximum_convert_fusion, f32[90]{0:T(128)S(1)} %get-tuple-element.41, f32[90]{0:T(128)S(1)} %get-tuple-element.42, f32[90]{0:T(128)S(1)} %get-tuple-element.35, f32[90]{0:T(128)S(1)} %get-tuple-element.36, f32[90]{0:T(128)S(1)} %get-tuple-element.37, ...), kind=kLoop, calls=%fused_computation.128 | loop fusion | flops 26525696 | bytes 59051176 | tf_op jit(solution)/shard_map/reduce_sum | solution.py:58
  310.1 4.3 copy.103
  315.5 15.2 %multiply_convert_fusion = (bf16[360,16384]{1,0:T(8,128)(2,1)}, f32[16384,360]{0,1:T(8,128)}) fusion(f32[360]{0:T(512)S(1)} %copy-done.16, bf16[90,360]{1,0:T(8,128)(2,1)S(1)} %copy-done.7, f32[90,16384]{1,0:T(8,128)S(1)} %bitcast.150, f32[90]{0:T(128)S(1)} %copy-done.15, f32[90]{0:T(128)S(1)} %copy-done.10, f32[16384]{0:T(1024)S(1)} %bitcast.169, ...), kind=kOutput, calls=%fused_computation.18 | convolution fusion | flops 1128038400 | bytes 41485712 | tf_op jit(solution)/shard_map/dot_general | solution.py:64
  330.7 20.6 %fusion.6 = bf16[360,16384]{1,0:T(8,128)(2,1)} fusion(f32[16384,360]{0,1:T(8,128)} %get-tuple-element.48, bf16[360,90]{0,1:T(8,128)(2,1)S(1)} %copy-done.8, bf16[90,16384]{1,0:T(8,128)(2,1)S(1)} %bitcast.165), kind=kOutput, calls=%fused_computation.16 | convolution fusion | flops 1173749760 | bytes 38403360 | tf_op jit(solution)/shard_map/dot_general | solution.py:75
  351.3 8.7 %convolution_multiply_fusion.1 = f32[90,360]{1,0:T(8,128)} fusion(bf16[360,16384]{1,0:T(8,128)(2,1)} %fusion.6, f32[90,16384]{1,0:T(8,128)S(1)} %bitcast.151, f32[90]{0:T(128)S(1)} %copy-done.15, f32[90]{0:T(128)S(1)} %copy-done.10, f32[16384]{0:T(1024)S(1)} %bitcast.170, f32[16384]{0:T(1024)S(1)} %bitcast.174), kind=kOutput, calls=%fused_computation.48 | convolution fusion | flops 1069088384 | bytes 17956112 | tf_op jit(solution)/shard_map/dot_general | solution.py:41
  360.0 10.5 %fusion.13 = (f32[16384]{0:T(1024)S(1)}, f32[16384,90]{0,1:T(8,128)}) fusion(f32[90,16384]{1,0:T(8,128)S(1)} %bitcast.152, f32[16384]{0:T(1024)S(1)} %bitcast.171, f32[16384]{0:T(1024)S(1)} %bitcast.175, f32[90]{0:T(128)S(1)} %copy-done.10, bf16[360,16384]{1,0:T(8,128)(2,1)} %fusion.6, bf16[90,360]{1,0:T(8,128)(2,1)S(1)} %copy-done.7), kind=kOutput, calls=%fused_computation.31 | convolution fusion | flops 1069039616 | bytes 23854728 | tf_op jit(solution)/shard_map/dot_general | solution.py:78
  370.6 8.6 %convolution_multiply_fusion.2 = f32[360,90]{0,1:T(8,128)} fusion(bf16[360,16384]{1,0:T(8,128)(2,1)} %get-tuple-element.47, bf16[90,16384]{1,0:T(8,128)(2,1)S(1)} %bitcast.166), kind=kOutput, calls=%fused_computation.49 | convolution fusion | flops 1061715584 | bytes 14875200 | tf_op jit(solution)/shard_map/dot_general | solution.py:41
  379.1 6.9 %fusion.10 = bf16[90,16384]{1,0:T(8,128)(2,1)S(1)} fusion(bf16[360,16384]{1,0:T(8,128)(2,1)} %get-tuple-element.47, bf16[360,90]{0,1:T(8,128)(2,1)S(1)} %copy-done.8, bf16[16384,90]{0,1:T(8,128)(2,1)S(1)} %fusion.7, f32[90]{0:T(128)S(1)} %copy-done.11), kind=kOutput, calls=%fused_computation.26 | convolution fusion | flops 1067581440 | bytes 17759880 | tf_op jit(solution)/shard_map/dot_general | solution.py:68
  392.7 6.2 %fusion.12 = f32[90,16384]{1,0:T(8,128)S(1)} fusion(f32[16384,90]{0,1:T(8,128)} %get-tuple-element.50, f32[90,16384]{1,0:T(8,128)} %bitcast.153, f32[16384]{0:T(1024)S(1)} %broadcast_multiply_fusion, f32[16384]{0:T(1024)S(1)} %broadcast_multiply_fusion.1, f32[16384]{0:T(1024)S(1)} %bitcast.172, f32[16384]{0:T(1024)S(1)} %bitcast.176), kind=kLoop, calls=%fused_computation.30 | loop fusion | flops 8847360 | bytes 17956864 | tf_op jit(solution)/shard_map/mul | solution.py:79
  398.9 7.0 %copy.108 = f32[12,8,32,512]{3,2,1,0:T(8,128)} copy(f32[12,8,32,512]{3,1,2,0:T(8,128)S(1)} %bitcast.158) | data formatting | bytes 12582912
  405.9 31.9 %multiply_reduce_fusion = (f32[90]{0:T(128)S(1)}, f32[90]{0:T(128)S(1)}, f32[90]{0:T(128)S(1)}, f32[90]{0:T(128)S(1)}, f32[90]{0:T(128)S(1)}, /*index=5*/f32[90]...) fusion(f32[90,34,514]{2,1,0:T(8,128)} %maximum_convert_fusion, f32[96,32,512]{2,1,0:T(8,128)} %bitcast.159), kind=kLoop, calls=%fused_computation.34 | loop fusion | flops 26541270 | bytes 58985640 | tf_op jit(solution)/shard_map/reduce_sum | solution.py:90
  437.8 67.0 %psum.23 = f32[9,90]{1,0:T(8,128)} all-reduce(f32[9,90]{1,0:T(8,128)S(1)} %broadcast_multiply_fusion.3), channel_id=1, replica_groups=mesh['face'=8,'tile'=16] {'face','tile'}, use_global_device_ids=true, to_apply=%region_23.24 | all-reduce | flops 810 | bytes 6480 | tf_op jit(solution)/shard_map/psum | solution.py:210
  504.8 77.2 %all-reduce.4.cloned.1.call-done = (f32[90,360]{1,0:T(8,128)}, f32[360,90]{0,1:T(8,128)}) async-done(((f32[90,360]{1,0:T(8,128)}, f32[360,90]{0,1:T(8,128)}), (f32[90,360]{1,0:T(8,128)}, f32[360,90]{0,1:T(8,128)})) %all-reduce.4.cloned.1.call-update) | async-done | bytes 259216 | tf_op jit(solution)/shard_map/psum | solution.py:210
  (134 shorter events, 78.7 us)
Async XLA Ops:
  7.2 20.5 %copy-start = (bf16[64,16,128]{2,1,0:T(8,128)(2,1)S(1)}, bf16[64,16,128]{2,1,0:T(8,128)(2,1)}, u32[]{:S(2)}) copy-start(bf16[64,16,128]{2,1,0:T(8,128)(2,1)} %param.16) | copy-start | bytes 786436
  8.0 48.0 %copy-start.17 = (s32[128]{0:T(128)S(1)}, s32[128]{0:T(128)}, u32[]{:S(2)}) copy-start(s32[128]{0:T(128)} %param.20) | copy-start | bytes 1540
  15.5 30.7 %all-to-all-start.1 = ((s32[128,1,2]{2,1,0:T(1,128)}), s32[128,1,2]{2,1,0:T(1,128)S(1)}, u32[]{:S(2)}, u32[]{:S(2)}) async-start(s32[128,1,2]{2,1,0:T(1,128)} %copy.79), calls=%async_computation.1 | async-start | bytes 131072 | tf_op jit(solution)/shard_map/all_to_all | solution.py:156
  46.2 28.7 %all-to-all-start.2 = ((bf16[128,2,16,128]{3,2,1,0:T(8,128)(2,1)}), bf16[128,2,16,128]{3,2,1,0:T(8,128)(2,1)S(1)}, u32[]{:S(2)}, u32[]{:S(2)}) async-start(bf16[128,2,16,128]{3,2,1,0:T(8,128)(2,1)} %scatter_fusion.1), calls=%async_computation.2 | async-start | bytes 2097152 | tf_op jit(solution)/shard_map/all_to_all | solution.py:155
  74.9 28.2 %all-to-all-start = ((s32[128,1,1]{2,1,0:T(1,128)}), s32[128,1,1]{2,1,0:T(1,128)S(1)}, u32[]{:S(2)}, u32[]{:S(2)}) async-start(s32[128,1,1]{2,1,0:T(1,128)} %copy.78), calls=%async_computation | async-start | bytes 131072 | tf_op jit(solution)/shard_map/all_to_all | solution.py:169
  79.8 60.8 %copy-start.12 = (bf16[16,90]{1,0:T(8,128)(2,1)S(1)}, bf16[16,90]{1,0:T(8,128)(2,1)}, u32[]{:S(2)}) copy-start(bf16[16,90]{1,0:T(8,128)(2,1)} %param.22) | copy-start | bytes 8644
  79.8 60.8 %copy-start.14 = (f32[90]{0:T(128)S(1)}, f32[90]{0:T(128)}, u32[]{:S(2)}) copy-start(f32[90]{0:T(128)} %param.23) | copy-start | bytes 1084
  103.1 23.4 %all-to-all-start.3 = ((bf16[128,16,128]{2,1,0:T(8,128)(2,1)}), bf16[128,16,128]{2,1,0:T(8,128)(2,1)S(1)}, u32[]{:S(2)}, u32[]{:S(2)}) async-start(bf16[128,16,128]{2,1,0:T(8,128)(2,1)} %scatter_fusion.3), calls=%async_computation.3 | async-start | bytes 1048576 | tf_op jit(solution)/shard_map/all_to_all | solution.py:168
  113.0 77.5 %all-gather.4.cloned.1.call-start = ((), (), s32[]{:S(2)}) async-start(), calls=%async_computation.4 | async-start | bytes 1566720 | tf_op jit(solution)/shard_map/all_gather | solution.py:179
  143.9 1.7 copy-start.3
  146.5 52.0 %copy-start.9 = (s32[8,4,3]{0,1,2:T(4,128)S(1)}, s32[8,4,3]{0,1,2:T(4,128)}, u32[]{:S(2)}) copy-start(s32[8,4,3]{0,1,2:T(4,128)} %param.21) | copy-start | bytes 1156
  147.3 90.7 %all-gather.6.cloned.1.call-start = ((), (), s32[]{:S(2)}) async-start(), calls=%async_computation.5 | async-start | bytes 3317760 | tf_op jit(solution)/shard_map/all_gather | solution.py:186
  198.3 6.8 %copy-start.13 = (f32[9,90]{1,0:T(8,128)S(1)}, f32[9,90]{1,0:T(8,128)}, u32[]{:S(2)}) copy-start(f32[9,90]{1,0:T(8,128)} %param.24) | copy-start | bytes 9724
  198.3 383.7 %all-reduce.4.cloned.1.call-start = ((), (), s32[]{:S(2)}) async-start(), calls=%async_computation.6 | async-start | bytes 589824 | tf_op jit(solution)/shard_map/psum | solution.py:210
  209.0 50.1 %collective-permute-start = (bf16[90,1,512]{2,0,1:T(8,128)(2,1)}, bf16[90,1,512]{2,0,1:T(8,128)(2,1)S(1)}, u32[]{:S(2)}, u32[]{:S(2)}) collective-permute-start(bf16[90,1,512]{2,0,1:T(8,128)(2,1)} %get-tuple-element.18), channel_id=1, source_target_pairs={{0,1},{1,2},{2,3},{3,4},{4,5},{5,6},{6,7},{7,8},{8,9},{9,10},{10,1... | collective-permute-start | bytes 276488 | tf_op jit(solution)/shard_map/ppermute | solution.py:21
  212.0 47.1 %collective-permute-start.1 = (bf16[90,1,512]{2,0,1:T(8,128)(2,1)}, bf16[90,1,512]{2,0,1:T(8,128)(2,1)}, u32[]{:S(2)}, u32[]{:S(2)}) collective-permute-start(bf16[90,1,512]{2,0,1:T(8,128)(2,1)} %get-tuple-element.19), channel_id=1, source_target_pairs={{1,0},{2,1},{3,2},{4,3},{5,4},{6,5},{7,6},{8,7},{9,8},{10,9},{11,1... | collective-permute-start | bytes 276488 | tf_op jit(solution)/shard_map/ppermute | solution.py:23
  256.5 0.8 copy-start.6
  306.5 8.0 %slice-start = ((s8[5898240]{0:T(1024)(128)(4,1)}), s8[4194304]{0:T(1024)(128)(4,1)S(1)}, s32[]{:S(2)}) async-start(s8[5898240]{0:T(1024)(128)(4,1)} %bitcast.154), calls=%async_computation.7 | async-start | bytes 8388608
  310.1 4.5 slice-start.1
  314.5 45.5 %copy-start.2 = (f32[12,8,32,512]{3,1,2,0:T(8,128)}, f32[12,8,32,512]{3,1,2,0:T(8,128)S(1)}, u32[]{:S(2)}) copy-start(f32[12,8,32,512]{3,1,2,0:T(8,128)S(1)} %copy.103) | copy-start | bytes 18874372
  314.5 1.0 copy-start.7
  314.5 0.9 copy-start.10
  314.5 0.9 copy-start.15
  314.5 0.9 copy-start.16
  315.4 15.2 %copy-start.4 = (bf16[12,8,32,512]{3,1,2,0:T(8,128)(2,1)S(1)}, bf16[12,8,32,512]{3,1,2,0:T(8,128)(2,1)}, u32[]{:S(2)}) copy-start(bf16[12,8,32,512]{3,1,2,0:T(8,128)(2,1)} %copy.107) | copy-start | bytes 9437188
  315.4 15.2 %copy-start.8 = (bf16[360,90]{0,1:T(8,128)(2,1)S(1)}, bf16[360,90]{0,1:T(8,128)(2,1)}, u32[]{:S(2)}) copy-start(bf16[360,90]{0,1:T(8,128)(2,1)} %param.29) | copy-start | bytes 194404
  360.0 10.6 %copy-start.5 = (bf16[12,8,32,512]{3,1,2,0:T(8,128)(2,1)S(1)}, bf16[12,8,32,512]{3,1,2,0:T(8,128)(2,1)}, u32[]{:S(2)}) copy-start(bf16[12,8,32,512]{3,1,2,0:T(8,128)(2,1)} %copy.107) | copy-start | bytes 9437188
  370.6 8.6 %copy-start.11 = (f32[90]{0:T(128)S(1)}, f32[90]{0:T(128)}, u32[]{:S(2)}) copy-start(f32[90]{0:T(128)} %param.30) | copy-start | bytes 1084
  405.9 179.2 %copy-start.1 = (bf16[64,16,128]{2,1,0:T(8,128)(2,1)S(1)}, bf16[64,16,128]{2,1,0:T(8,128)(2,1)}, u32[]{:S(2)}) copy-start(bf16[64,16,128]{2,1,0:T(8,128)(2,1)} %param.16) | copy-start | bytes 786436
Sparse Core Ops, SparseCore 0:
  147.4 43.0 all-gather.3
  198.4 39.5 all-gather.5
  437.9 144.0 all-reduce.3
where the time goes:
time: 601 us; the launch traced here: 592 us
  waiting for transfers between devices  132 us (22%)
  local copies, waits for them, and re-layouts  130 us (22%)
  other arithmetic  107 us (18%)
  blocking collectives  90.3 us (15%)
  matrix products  76 us (13%)
  starting transfers between devices  41.3 us (7%)
  between operations  14.6 us (2%)
    psum x1, waiting for transfers between devices, per_device(): lax.psum((grad_one, grad_two, grad_kernel), ('face', 'tile'))  77.2 us
    psum x1, blocking collectives, per_device(): lax.psum((grad_one, grad_two, grad_kernel), ('face', 'tile'))  67 us
    reduce_sum x1, other arithmetic, strip_work(): mean_val = jnp.mean(flat, axis=0, keepdims=True)  34.9 us
    unnamed x54, local copies, waits for them, and re-layouts  33.3 us
    reduce_sum x1, other arithmetic, strip_work(): kernel_rows.append(jnp.sum(back_grid * window, axis=(1, 2)))  31.9 us
    all_gather x1, waiting for transfers between devices, per_device(): lax.all_gather(own_lines.reshape(-1), 'face', axis=0, tiled=True)  24 us
    all_gather x1, blocking collectives, per_device(): lax.all_gather(edge_cols.reshape(-1), 'tile', axis=0, tiled=True)  23.3 us
    dot_general x1, matrix products, strip_work(): back_hidden = jnp.dot(w_two, cot_flat, preferred_element_type=jnp.float32)  20.6 us
  transfers between devices with their start and end apart: 9, of which 5 were waited for; matrix products, arithmetic and copies ran while one was open for 16% of the time, Pallas kernels for 0%

commit v1 on v0

--- a/solution.py
+++ b/solution.py
@@ -183,9 +183,12 @@
         rows_face.reshape(tile_count, chan_count, line_len),
         cols_face.reshape(tile_count, 2, chan_count, row_count),
     )
-    all_lines = lax.all_gather(own_lines.reshape(-1), "face", axis=0, tiled=True).reshape(
-        face_count, 4, chan_count, line_len
-    )
+    all_lines = jnp.concatenate(
+        jax.lax.all_to_all(
+            jnp.stack(jax.lax.axis_size("face") * [own_lines.reshape(-1)], 0), "face", 0, 0
+        ),
+        0,
+    ).reshape(face_count, 4, chan_count, line_len)
     face_link = face_links[face_at]
     picked = all_lines[face_link[:, 0], face_link[:, 1]]
     picked = jnp.where(face_link[:, 2][:, None, None] == 1, picked[:, :, ::-1], picked)

time: 601 us -> 684 us (1.14)
  other arithmetic: 107 us -> 162 us
  local copies, waits for them, and re-layouts: 130 us -> 152 us
    another operation x0 -> x1, other arithmetic: none -> 54.4 us  [per_device(): jnp.stack(jax.lax.axis_size('face') * [own_lines.reshape(-1)], 0)]
    all_gather x1 -> x0, waiting for transfers between devices: 24 us -> none  [per_device(): lax.all_gather(own_lines.reshape(-1), 'face', axis=0, tiled=True)]
    all_to_all x0 -> x1, waiting for transfers between devices: none -> 20.4 us  [per_device(): jax.lax.all_to_all(jnp.stack(jax.lax.axis_size('face') * [own_lines.resha...]
    unnamed x54 -> x56, local copies, waits for them, and re-layouts: 33.3 us -> 47.2 us
    another operation x2 -> x6, local copies, waits for them, and re-layouts: 1.73 us -> 12.7 us  [the longest x3 8.25 us: per_device(): jnp.stack(jax.lax.axis_size('face') * [own_lines.reshape(-1)], 0)]
    reshape x2 -> x0, local copies, waits for them, and re-layouts: 7.6 us -> none  [the longest x1 5.65 us: per_device(): lax.all_gather(own_lines.reshape(-1), 'face', axis=0, tiled=True)]
  transfers between devices with their start and end apart: 9 -> 9, of which waited for: 5 -> 5; matrix products, arithmetic and copies ran while one was open for 16% -> 15% of each run, Pallas kernels for 0% -> 0%
where the time goes in v1:
time: 684 us; the launch traced here: 675 us
  other arithmetic  162 us (24%)
  local copies, waits for them, and re-layouts  152 us (22%)
  waiting for transfers between devices  128 us (19%)
  blocking collectives  96.1 us (14%)
  matrix products  76.1 us (11%)
  starting transfers between devices  45.6 us (7%)
  between operations  14.8 us (2%)
    psum x1, waiting for transfers between devices, per_device(): lax.psum((grad_one, grad_two, grad_kernel), ('face', 'tile'))  76.5 us
    psum x1, blocking collectives, per_device(): lax.psum((grad_one, grad_two, grad_kernel), ('face', 'tile'))  72.7 us
    another operation x1, other arithmetic, per_device(): jnp.stack(jax.lax.axis_size('face') * [own_lines.reshape(-1)], 0)  54.4 us
    unnamed x56, local copies, waits for them, and re-layouts  47.2 us
    reduce_sum x1, other arithmetic, strip_work(): mean_val = jnp.mean(flat, axis=0, keepdims=True)  34.7 us
    reduce_sum x1, other arithmetic, strip_work(): kernel_rows.append(jnp.sum(back_grid * window, axis=(1, 2)))  31.8 us
    all_gather x1, blocking collectives, per_device(): lax.all_gather(edge_cols.reshape(-1), 'tile', axis=0, tiled=True)  23.4 us
    dot_general x1, matrix products, strip_work(): back_hidden = jnp.dot(w_two, cot_flat, preferred_element_type=jnp.float32)  20.6 us
  transfers between devices with their start and end apart: 9, of which 5 were waited for; matrix products, arithmetic and copies ran while one was open for 15% of the time, Pallas kernels for 0%

profile of v1, /device:TPU:1, one launch (start us, length us, event | category | flops | bytes accessed | tf_op | source)
XLA Modules:
  0.0 674.7 jit_solution(9910259348530299273)
XLA Ops:
  8.4 6.4 scatter_fusion
  15.5 11.5 %all-to-all-start.1 = ((s32[128,1,2]{2,1,0:T(1,128)}), s32[128,1,2]{2,1,0:T(1,128)S(1)}, u32[]{:S(2)}, u32[]{:S(2)}) async-start(s32[128,1,2]{2,1,0:T(1,128)} %copy.85), calls=%async_computation.1 | async-start | bytes 131072 | tf_op jit(solution)/shard_map/all_to_all | solution.py:156
  33.0 13.3 %scatter_fusion.1 = bf16[128,2,16,128]{3,2,1,0:T(8,128)(2,1)} fusion(bf16[128,2,16,128]{3,2,1,0:T(8,128)(2,1)} %broadcast_in_dim.46, s32[128]{0:T(128)S(1)} %fusion.33, bf16[128,16,128]{2,1,0:T(8,128)(2,1)S(1)} %convolution_convert_fusion), kind=kCustom, calls=%fused_computation.4 | custom fusion | bytes 1573888 | tf_op jit(solution)/shard_map/scatter | solution.py:149
  46.2 9.8 %all-to-all-start.2 = ((bf16[128,2,16,128]{3,2,1,0:T(8,128)(2,1)}), bf16[128,2,16,128]{3,2,1,0:T(8,128)(2,1)S(1)}, u32[]{:S(2)}, u32[]{:S(2)}) async-start(bf16[128,2,16,128]{3,2,1,0:T(8,128)(2,1)} %scatter_fusion.1), calls=%async_computation.2 | async-start | bytes 2097152 | tf_op jit(solution)/shard_map/all_to_all | solution.py:155
  59.2 15.7 %all-to-all-done.2 = bf16[128,2,16,128]{3,2,1,0:T(8,128)(2,1)S(1)} async-done(((bf16[128,2,16,128]{3,2,1,0:T(8,128)(2,1)}), bf16[128,2,16,128]{3,2,1,0:T(8,128)(2,1)S(1)}, u32[]{:S(2)}, u32[]{:S(2)}) %all-to-all-start.2) | async-done | bytes 1048608 | tf_op jit(solution)/shard_map/all_to_all | solution.py:155
  74.9 4.5 all-to-all-start
  79.8 9.2 %scatter_fusion.2 = f32[128,16,128]{2,1,0:T(8,128)S(1)} fusion(f32[128,16,128]{2,1,0:T(8,128)S(1)} %broadcast_in_dim.43, s32[256]{0:T(256)S(1)} %bitcast.185, f32[256,16,128]{2,1,0:T(8,128)S(1)} %bitcast_convert_fusion), kind=kCustom, calls=%fused_computation.5 | custom fusion | flops 524288 | bytes 6292480 | tf_op jit(solution)/shard_map/scatter-add | solution.py:159
  90.0 13.2 %scatter_fusion.3 = bf16[128,16,128]{2,1,0:T(8,128)(2,1)} fusion(bf16[128,16,128]{2,1,0:T(8,128)(2,1)} %broadcast.198.clone, s32[128]{0:T(128)S(1)} %get-tuple-element.46, bf16[128,16,128]{2,1,0:T(8,128)(2,1)S(1)} %convert_element_type.45), kind=kCustom, calls=%fused_computation.6 | custom fusion | bytes 1573376 | tf_op jit(solution)/shard_map/scatter | solution.py:165
  103.1 9.8 %all-to-all-start.3 = ((bf16[128,16,128]{2,1,0:T(8,128)(2,1)}), bf16[128,16,128]{2,1,0:T(8,128)(2,1)S(1)}, u32[]{:S(2)}, u32[]{:S(2)}) async-start(bf16[128,16,128]{2,1,0:T(8,128)(2,1)} %scatter_fusion.3), calls=%async_computation.3 | async-start | bytes 1048576 | tf_op jit(solution)/shard_map/all_to_all | solution.py:168
  115.6 11.0 %all-to-all-done.3 = bf16[128,16,128]{2,1,0:T(8,128)(2,1)S(1)} async-done(((bf16[128,16,128]{2,1,0:T(8,128)(2,1)}), bf16[128,16,128]{2,1,0:T(8,128)(2,1)S(1)}, u32[]{:S(2)}, u32[]{:S(2)}) %all-to-all-start.3) | async-done | bytes 524320 | tf_op jit(solution)/shard_map/all_to_all | solution.py:168
  127.4 13.2 %scatter_fusion.4 = bf16[128,16,128]{2,1,0:T(8,128)(2,1)} fusion(bf16[128,16,128]{2,1,0:T(8,128)(2,1)} %broadcast.198, s32[128]{0:T(128)S(1)} %fusion.31, bf16[128,16,128]{2,1,0:T(8,128)(2,1)S(1)} %all-to-all-done.3), kind=kCustom, calls=%fused_computation.7 | custom fusion | bytes 1573376 | tf_op jit(solution)/shard_map/scatter | solution.py:171
  154.1 23.4 %all-gather = bf16[16,1,5760]{2,1,0:T(2,128)(2,1)} all-gather(bf16[1,1,5760]{2,1,0:T(2,128)(2,1)S(1)} %reshape.284), channel_id=1, replica_groups=mesh['face'=8,'tile'=16] {'tile'}, dimensions={0}, use_global_device_ids=true | all-gather | bytes 195840 | tf_op jit(solution)/shard_map/all_gather | solution.py:180
  198.4 5.7 stack.44
  204.6 54.4 %reduce.13 = bf16[8,184320]{1,0:T(8,128)(2,1)} reduce(bf16[8,1,184320]{2,1,0:T(2,128)(2,1)} %stack.44, bf16[]{:T(256)} %broadcast.331), dimensions={1}, to_apply=%stack.44.reduce_sub_computation | reduce | bytes 5898242 | tf_op jit(solution)/shard_map/stack | solution.py:188
  259.0 6.1 reshape.303
  285.5 20.4 %all-to-all-done.4 = bf16[8,2,92160]{2,1,0:T(2,128)(2,1)} async-done(((bf16[8,2,92160]{2,1,0:T(2,128)(2,1)}), bf16[8,2,92160]{2,1,0:T(2,128)(2,1)}, u32[]{:S(2)}, u32[]{:S(2)}) %all-to-all-start.4) | async-done | bytes 2949152 | tf_op jit(solution)/shard_map/all_to_all | solution.py:187
  305.9 7.6 %reshape.304 = bf16[8,1,184320]{2,1,0:T(2,128)(2,1)} reshape(bf16[8,2,92160]{2,1,0:T(2,128)(2,1)} %all-to-all-done.4) | data formatting | bytes 5898240
  313.5 4.9 copy.96
  324.3 8.5 %rev.3 = bf16[4,90,512]{2,1,0:T(8,128)(2,1)} reverse(bf16[4,90,512]{2,1,0:T(8,128)(2,1)} %gather_fusion.1), dimensions={2} | reverse | bytes 737280 | tf_op jit(solution)/shard_map/rev | solution.py:194
  340.2 8.9 %maximum_convert_fusion = f32[90,34,514]{2,1,0:T(8,128)} fusion(bf16[90,34,1]{2,1,0:T(8,128)(2,1)} %copy.103, bf16[90,1,512]{2,1,0:T(2,128)(2,1)S(1)} %copy.100, bf16[90,32,512]{2,1,0:T(8,128)(2,1)} %slice.204, bf16[90,1,512]{2,1,0:T(2,128)(2,1)} %copy.99, bf16[90,34,1]{2,1,0:T(8,128)(2,1)} %copy.102), kind=kLoop, calls=%fused_computation.45 | loop fusion | flops 15728400 | bytes 9437040 | tf_op jit(solution)/shard_map/convert_element_type | solution.py:50
  349.1 34.7 %fusion.38 = (f32[32,512]{1,0:T(8,128)S(1)}, f32[90,32,512]{2,1,0:T(8,128)}) fusion(f32[90,34,514]{2,1,0:T(8,128)} %maximum_convert_fusion, f32[90]{0:T(128)S(1)} %get-tuple-element.41, f32[90]{0:T(128)S(1)} %get-tuple-element.42, f32[90]{0:T(128)S(1)} %get-tuple-element.35, f32[90]{0:T(128)S(1)} %get-tuple-element.36, f32[90]{0:T(128)S(1)} %get-tuple-element.37, ...), kind=kLoop, calls=%fused_computation.128 | loop fusion | flops 26525696 | bytes 59051176 | tf_op jit(solution)/shard_map/reduce_sum | solution.py:58
  392.7 15.2 %multiply_convert_fusion = (bf16[360,16384]{1,0:T(8,128)(2,1)}, f32[16384,360]{0,1:T(8,128)}) fusion(f32[360]{0:T(512)S(1)} %copy-done.16, bf16[90,360]{1,0:T(8,128)(2,1)S(1)} %copy-done.7, f32[90,16384]{1,0:T(8,128)S(1)} %bitcast.151, f32[90]{0:T(128)S(1)} %copy-done.15, f32[90]{0:T(128)S(1)} %copy-done.10, f32[16384]{0:T(1024)S(1)} %bitcast.171, ...), kind=kOutput, calls=%fused_computation.18 | convolution fusion | flops 1128038400 | bytes 41485712 | tf_op jit(solution)/shard_map/dot_general | solution.py:64
  407.9 20.6 %fusion.6 = bf16[360,16384]{1,0:T(8,128)(2,1)} fusion(f32[16384,360]{0,1:T(8,128)} %get-tuple-element.48, bf16[360,90]{0,1:T(8,128)(2,1)S(1)} %copy-done.8, bf16[90,16384]{1,0:T(8,128)(2,1)S(1)} %bitcast.166), kind=kOutput, calls=%fused_computation.16 | convolution fusion | flops 1173749760 | bytes 38403360 | tf_op jit(solution)/shard_map/dot_general | solution.py:75
  428.6 8.7 %convolution_multiply_fusion.1 = f32[90,360]{1,0:T(8,128)} fusion(bf16[360,16384]{1,0:T(8,128)(2,1)} %fusion.6, f32[90,16384]{1,0:T(8,128)S(1)} %bitcast.152, f32[90]{0:T(128)S(1)} %copy-done.15, f32[90]{0:T(128)S(1)} %copy-done.10, f32[16384]{0:T(1024)S(1)} %bitcast.172, f32[16384]{0:T(1024)S(1)} %bitcast.176), kind=kOutput, calls=%fused_computation.48 | convolution fusion | flops 1069088384 | bytes 17956112 | tf_op jit(solution)/shard_map/dot_general | solution.py:41
  437.3 10.5 %fusion.13 = (f32[16384]{0:T(1024)S(1)}, f32[16384,90]{0,1:T(8,128)}) fusion(f32[90,16384]{1,0:T(8,128)S(1)} %bitcast.153, f32[16384]{0:T(1024)S(1)} %bitcast.173, f32[16384]{0:T(1024)S(1)} %bitcast.177, f32[90]{0:T(128)S(1)} %copy-done.10, bf16[360,16384]{1,0:T(8,128)(2,1)} %fusion.6, bf16[90,360]{1,0:T(8,128)(2,1)S(1)} %copy-done.7), kind=kOutput, calls=%fused_computation.31 | convolution fusion | flops 1069039616 | bytes 23854728 | tf_op jit(solution)/shard_map/dot_general | solution.py:78
  447.8 8.6 %convolution_multiply_fusion.2 = f32[360,90]{0,1:T(8,128)} fusion(bf16[360,16384]{1,0:T(8,128)(2,1)} %get-tuple-element.47, bf16[90,16384]{1,0:T(8,128)(2,1)S(1)} %bitcast.167), kind=kOutput, calls=%fused_computation.49 | convolution fusion | flops 1061715584 | bytes 14875200 | tf_op jit(solution)/shard_map/dot_general | solution.py:41
  456.4 6.9 %fusion.10 = bf16[90,16384]{1,0:T(8,128)(2,1)S(1)} fusion(bf16[360,16384]{1,0:T(8,128)(2,1)} %get-tuple-element.47, bf16[360,90]{0,1:T(8,128)(2,1)S(1)} %copy-done.8, bf16[16384,90]{0,1:T(8,128)(2,1)S(1)} %fusion.7, f32[90]{0:T(128)S(1)} %copy-done.11), kind=kOutput, calls=%fused_computation.26 | convolution fusion | flops 1067581440 | bytes 17759880 | tf_op jit(solution)/shard_map/dot_general | solution.py:68
  470.2 6.2 fusion.12
  476.4 7.0 %copy.119 = f32[12,8,32,512]{3,2,1,0:T(8,128)} copy(f32[12,8,32,512]{3,1,2,0:T(8,128)S(1)} %bitcast.159) | data formatting | bytes 12582912
  483.4 31.8 %multiply_reduce_fusion = (f32[90]{0:T(128)S(1)}, f32[90]{0:T(128)S(1)}, f32[90]{0:T(128)S(1)}, f32[90]{0:T(128)S(1)}, f32[90]{0:T(128)S(1)}, /*index=5*/f32[90]...) fusion(f32[90,34,514]{2,1,0:T(8,128)} %maximum_convert_fusion, f32[96,32,512]{2,1,0:T(8,128)} %bitcast.160), kind=kLoop, calls=%fused_computation.34 | loop fusion | flops 26541270 | bytes 58985640 | tf_op jit(solution)/shard_map/reduce_sum | solution.py:90
  515.2 72.7 %psum.23 = f32[9,90]{1,0:T(8,128)} all-reduce(f32[9,90]{1,0:T(8,128)S(1)} %broadcast_multiply_fusion.3), channel_id=1, replica_groups=mesh['face'=8,'tile'=16] {'face','tile'}, use_global_device_ids=true, to_apply=%region_23.24 | all-reduce | flops 810 | bytes 6480 | tf_op jit(solution)/shard_map/psum | solution.py:213
  588.0 76.5 %all-reduce.4.cloned.1.call-done = (f32[90,360]{1,0:T(8,128)}, f32[360,90]{0,1:T(8,128)}) async-done(((f32[90,360]{1,0:T(8,128)}, f32[360,90]{0,1:T(8,128)}), (f32[90,360]{1,0:T(8,128)}, f32[360,90]{0,1:T(8,128)})) %all-reduce.4.cloned.1.call-update) | async-done | bytes 259216 | tf_op jit(solution)/shard_map/psum | solution.py:213
  (139 shorter events, 102.9 us)
Async XLA Ops:
  7.2 20.5 %copy-start = (bf16[64,16,128]{2,1,0:T(8,128)(2,1)S(1)}, bf16[64,16,128]{2,1,0:T(8,128)(2,1)}, u32[]{:S(2)}) copy-start(bf16[64,16,128]{2,1,0:T(8,128)(2,1)} %param.16) | copy-start | bytes 786436
  8.0 48.0 %copy-start.17 = (s32[128]{0:T(128)S(1)}, s32[128]{0:T(128)}, u32[]{:S(2)}) copy-start(s32[128]{0:T(128)} %param.20) | copy-start | bytes 1540
  15.5 30.7 %all-to-all-start.1 = ((s32[128,1,2]{2,1,0:T(1,128)}), s32[128,1,2]{2,1,0:T(1,128)S(1)}, u32[]{:S(2)}, u32[]{:S(2)}) async-start(s32[128,1,2]{2,1,0:T(1,128)} %copy.85), calls=%async_computation.1 | async-start | bytes 131072 | tf_op jit(solution)/shard_map/all_to_all | solution.py:156
  46.2 28.7 %all-to-all-start.2 = ((bf16[128,2,16,128]{3,2,1,0:T(8,128)(2,1)}), bf16[128,2,16,128]{3,2,1,0:T(8,128)(2,1)S(1)}, u32[]{:S(2)}, u32[]{:S(2)}) async-start(bf16[128,2,16,128]{3,2,1,0:T(8,128)(2,1)} %scatter_fusion.1), calls=%async_computation.2 | async-start | bytes 2097152 | tf_op jit(solution)/shard_map/all_to_all | solution.py:155
  74.9 28.2 %all-to-all-start = ((s32[128,1,1]{2,1,0:T(1,128)}), s32[128,1,1]{2,1,0:T(1,128)S(1)}, u32[]{:S(2)}, u32[]{:S(2)}) async-start(s32[128,1,1]{2,1,0:T(1,128)} %copy.84), calls=%async_computation | async-start | bytes 131072 | tf_op jit(solution)/shard_map/all_to_all | solution.py:169
  79.8 60.8 %copy-start.12 = (bf16[16,90]{1,0:T(8,128)(2,1)S(1)}, bf16[16,90]{1,0:T(8,128)(2,1)}, u32[]{:S(2)}) copy-start(bf16[16,90]{1,0:T(8,128)(2,1)} %param.22) | copy-start | bytes 8644
  79.8 60.8 %copy-start.14 = (f32[90]{0:T(128)S(1)}, f32[90]{0:T(128)}, u32[]{:S(2)}) copy-start(f32[90]{0:T(128)} %param.23) | copy-start | bytes 1084
  103.1 23.4 %all-to-all-start.3 = ((bf16[128,16,128]{2,1,0:T(8,128)(2,1)}), bf16[128,16,128]{2,1,0:T(8,128)(2,1)S(1)}, u32[]{:S(2)}, u32[]{:S(2)}) async-start(bf16[128,16,128]{2,1,0:T(8,128)(2,1)} %scatter_fusion.3), calls=%async_computation.3 | async-start | bytes 1048576 | tf_op jit(solution)/shard_map/all_to_all | solution.py:168
  113.0 77.6 %all-gather.3.cloned.1.call-start = ((), (), s32[]{:S(2)}) async-start(), calls=%async_computation.5 | async-start | bytes 1566720 | tf_op jit(solution)/shard_map/all_gather | solution.py:179
  143.9 1.7 copy-start.3
  259.0 10.6 %copy-start.9 = (s32[8,4,3]{0,1,2:T(4,128)S(1)}, s32[8,4,3]{0,1,2:T(4,128)}, u32[]{:S(2)}) copy-start(s32[8,4,3]{0,1,2:T(4,128)} %param.21) | copy-start | bytes 1156
  265.1 40.8 %all-to-all-start.4 = ((bf16[8,2,92160]{2,1,0:T(2,128)(2,1)}), bf16[8,2,92160]{2,1,0:T(2,128)(2,1)}, u32[]{:S(2)}, u32[]{:S(2)}) async-start(bf16[8,2,92160]{2,1,0:T(2,128)(2,1)} %reshape.303), calls=%async_computation.4 | async-start | bytes 5898240 | tf_op jit(solution)/shard_map/all_to_all | solution.py:187
  269.6 6.7 copy-start.13
  269.6 394.9 %all-reduce.4.cloned.1.call-start = ((), (), s32[]{:S(2)}) async-start(), calls=%async_computation.6 | async-start | bytes 589824 | tf_op jit(solution)/shard_map/psum | solution.py:213
  280.1 56.4 %collective-permute-start = (bf16[90,1,512]{2,0,1:T(8,128)(2,1)}, bf16[90,1,512]{2,0,1:T(8,128)(2,1)S(1)}, u32[]{:S(2)}, u32[]{:S(2)}) collective-permute-start(bf16[90,1,512]{2,0,1:T(8,128)(2,1)} %get-tuple-element.18), channel_id=1, source_target_pairs={{0,1},{1,2},{2,3},{3,4},{4,5},{5,6},{6,7},{7,8},{8,9},{9,10},{10,1... | collective-permute-start | bytes 276488 | tf_op jit(solution)/shard_map/ppermute | solution.py:21
  283.1 53.5 %collective-permute-start.1 = (bf16[90,1,512]{2,0,1:T(8,128)(2,1)}, bf16[90,1,512]{2,0,1:T(8,128)(2,1)}, u32[]{:S(2)}, u32[]{:S(2)}) collective-permute-start(bf16[90,1,512]{2,0,1:T(8,128)(2,1)} %get-tuple-element.19), channel_id=1, source_target_pairs={{1,0},{2,1},{3,2},{4,3},{5,4},{6,5},{7,6},{8,7},{9,8},{10,9},{11,1... | collective-permute-start | bytes 276488 | tf_op jit(solution)/shard_map/ppermute | solution.py:23
  334.0 0.8 copy-start.6
  383.8 8.0 %slice-start = ((s8[5898240]{0:T(1024)(128)(4,1)}), s8[4194304]{0:T(1024)(128)(4,1)S(1)}, s32[]{:S(2)}) async-start(s8[5898240]{0:T(1024)(128)(4,1)} %bitcast.155), calls=%async_computation.7 | async-start | bytes 8388608
  387.4 4.5 slice-start.1
  391.7 45.6 %copy-start.2 = (f32[12,8,32,512]{3,1,2,0:T(8,128)}, f32[12,8,32,512]{3,1,2,0:T(8,128)S(1)}, u32[]{:S(2)}) copy-start(f32[12,8,32,512]{3,1,2,0:T(8,128)S(1)} %copy.114) | copy-start | bytes 18874372
  391.7 1.0 copy-start.7
  391.7 0.9 copy-start.10
  391.8 0.9 copy-start.15
  391.8 0.9 copy-start.16
  392.7 15.2 %copy-start.4 = (bf16[12,8,32,512]{3,1,2,0:T(8,128)(2,1)S(1)}, bf16[12,8,32,512]{3,1,2,0:T(8,128)(2,1)}, u32[]{:S(2)}) copy-start(bf16[12,8,32,512]{3,1,2,0:T(8,128)(2,1)} %copy.118) | copy-start | bytes 9437188
  392.7 15.2 %copy-start.8 = (bf16[360,90]{0,1:T(8,128)(2,1)S(1)}, bf16[360,90]{0,1:T(8,128)(2,1)}, u32[]{:S(2)}) copy-start(bf16[360,90]{0,1:T(8,128)(2,1)} %param.29) | copy-start | bytes 194404
  437.3 10.6 %copy-start.5 = (bf16[12,8,32,512]{3,1,2,0:T(8,128)(2,1)S(1)}, bf16[12,8,32,512]{3,1,2,0:T(8,128)(2,1)}, u32[]{:S(2)}) copy-start(bf16[12,8,32,512]{3,1,2,0:T(8,128)(2,1)} %copy.118) | copy-start | bytes 9437188
  447.8 8.6 %copy-start.11 = (f32[90]{0:T(128)S(1)}, f32[90]{0:T(128)}, u32[]{:S(2)}) copy-start(f32[90]{0:T(128)} %param.30) | copy-start | bytes 1084
  483.3 184.3 %copy-start.1 = (bf16[64,16,128]{2,1,0:T(8,128)(2,1)S(1)}, bf16[64,16,128]{2,1,0:T(8,128)(2,1)}, u32[]{:S(2)}) copy-start(bf16[64,16,128]{2,1,0:T(8,128)(2,1)} %param.16) | copy-start | bytes 786436
Sparse Core Ops, SparseCore 0:
  147.4 43.0 all-gather.2
  515.3 149.1 all-reduce.3
